TPU v7x, 32 devices: a whole 2x2x4 slice. The times are simulated.
32 devices in a mesh: pipe: 2 (over x), row: 8 (over z, core), col: 2 (over y).
Axes of the slice: x: 2, y: 2, z: 4, core: 2. Of those that a mesh axis runs over, the one named last changes fastest.
Arguments:
- inputs: bfloat16 [4, 8, 1024, 512], P(None, 'row', 'col'), may hold values from -6 to 6
- first_gain: float32 [2, 512], P('pipe'), may hold values from 0.5 to 1.5
- first_shift: float32 [2, 512], P('pipe'), may hold values from -1.75 to 1.75
- qkv_weight: bfloat16 [2, 3, 512, 512], P('pipe', None, 'row', 'col'), may hold values from -0.25 to 0.25
- query_bias: float32 [2, 512], P('pipe', 'col'), may hold values from -3 to 3
- value_bias: float32 [2, 512], P('pipe', 'col'), may hold values from -1.75 to 1.75
- proj_weight: bfloat16 [2, 512, 512], P('pipe', 'col', 'row'), may hold values from -1 to 1
- proj_bias: float32 [2, 512], P('pipe'), may hold values from -1.75 to 1.75
- second_gain: float32 [2, 512], P('pipe'), may hold values from 0.5 to 1.5
- second_shift: float32 [2, 512], P('pipe'), may hold values from -1.75 to 1.75
- up_weight: bfloat16 [2, 512, 2048], P('pipe', 'row', 'col'), may hold values from -0.25 to 0.25
- up_bias: float32 [2, 2048], P('pipe', 'col'), may hold values from -3 to 3
- down_weight: bfloat16 [2, 2048, 512], P('pipe', 'col', 'row'), may hold values from -0.125 to 0.125
- down_bias: float32 [2, 512], P('pipe'), may hold values from -1.75 to 1.75
- cotangent: bfloat16 [4, 8, 1024, 512], P(None, 'row', 'col'), may hold values from -6 to 6
- live_clips: int32 [4, 8], P(None, 'row'), may hold values 0 or 1
Outputs:
- states: bfloat16 [2, 4, 8, 1024, 512], P('pipe', None, 'row', 'col')
- state_grads: float32 [2, 4, 8, 1024, 512], P('pipe', None, 'row', 'col')
- grad_first_gain: float32 [2, 512], P('pipe')
- grad_first_shift: float32 [2, 512], P('pipe')
- grad_qkv_weight: float32 [2, 3, 512, 512], P('pipe', None, 'row', 'col')
- grad_query_bias: float32 [2, 512], P('pipe', 'col')
- grad_value_bias: float32 [2, 512], P('pipe', 'col')
- grad_proj_weight: float32 [2, 512, 512], P('pipe', 'col', 'row')
- grad_proj_bias: float32 [2, 512], P('pipe')
- grad_second_gain: float32 [2, 512], P('pipe')
- grad_second_shift: float32 [2, 512], P('pipe')
- grad_up_weight: float32 [2, 512, 2048], P('pipe', 'row', 'col')
- grad_up_bias: float32 [2, 2048], P('pipe', 'col')
- grad_down_weight: float32 [2, 2048, 512], P('pipe', 'col', 'row')
- grad_down_bias: float32 [2, 512], P('pipe')
All inputs are finite; a program needn't handle non-finite values. No bound on the sum of `live_clips` on one device may be relied on, other than what follows from the above.
Results may differ from a plain program's by a relative error of at most 0.015.
Values may be sent and summed in bfloat16 or wider, within the bound.
A program may use at most 192 MiB of HBM per device.

v0:
```python
import math
import jax
import jax.numpy as jnp
from jax import lax
from jax.sharding import PartitionSpec as P

HD = 64
epsilon = 1e-05


def from_behind(value, axis, steps):
    count = lax.axis_size(axis)
    first, last = (max(0, -steps), min(count, count - steps))
    return lax.ppermute(value, axis, [(source, source + steps) for source in range(first, last)])


def exact_gelu(values):
    return jax.nn.gelu(values, approximate=False)


def spread_features(normed):
    return lax.all_gather(normed, "col", axis=0, tiled=True)


def sum_columns(partial_rows):
    return lax.psum_scatter(partial_rows, "col", scatter_dimension=0, tiled=True)


def spread_grads(grad_low):
    return lax.all_gather(grad_low, "col", axis=0, tiled=True)


def sum_grad_columns(partial_rows):
    return lax.psum_scatter(partial_rows, "col", scatter_dimension=0, tiled=True)


def norm_forward(values, gain, shift):
    row_mean = jnp.mean(values, axis=-1, keepdims=True)
    row_var = jnp.mean(jnp.square(values - row_mean), axis=-1, keepdims=True)
    inv_std = lax.rsqrt(row_var + epsilon)
    centered = (values - row_mean) * inv_std
    return (centered, inv_std[:, 0], (centered * gain + shift).astype(jnp.bfloat16))


def norm_backward(grad_norm, centered, inv_std, gain):
    grad_gain = jnp.sum(grad_norm * centered, axis=0)
    grad_shift = jnp.sum(grad_norm, axis=0)
    scaled = grad_norm * gain
    first = jnp.mean(scaled, axis=-1, keepdims=True)
    second = jnp.mean(scaled * centered, axis=-1, keepdims=True)
    grad_in = inv_std[:, None] * (scaled - first - centered * second)
    return (grad_in, grad_gain, grad_shift)


def attention_probs(query_heads, key_heads):
    score_scale = 1.0 / math.sqrt(HD)
    scores = (
        jnp.einsum("qhd,khd->hqk", query_heads, key_heads, preferred_element_type=jnp.float32)
        * score_scale
    )
    return jax.nn.softmax(scores, axis=-1)


def layer_forward(values, weights, params):
    qkv_full, proj_full, up_full, down_full = weights
    (
        gain_one,
        shift_one,
        query_bias,
        value_bias,
        proj_bias,
        gain_two,
        shift_two,
        up_bias,
        down_bias,
    ) = params
    head_count = qkv_full.shape[2] // HD
    centered_one, inv_one, normed_one = norm_forward(values, gain_one, shift_one)
    attn_input = spread_features(normed_one)
    frame_count = attn_input.shape[0]
    projected = jnp.einsum("sd,jde->jse", attn_input, qkv_full, preferred_element_type=jnp.float32)
    query_heads = (
        (projected[0] + query_bias).astype(jnp.bfloat16).reshape(frame_count, head_count, HD)
    )
    key_heads = projected[1].astype(jnp.bfloat16).reshape(frame_count, head_count, HD)
    value_heads = (
        (projected[2] + value_bias).astype(jnp.bfloat16).reshape(frame_count, head_count, HD)
    )
    softmax_out = attention_probs(query_heads, key_heads)
    context = jnp.einsum(
        "hqk,khd->qhd",
        softmax_out.astype(jnp.bfloat16),
        value_heads,
        preferred_element_type=jnp.float32,
    )
    context = context.reshape(frame_count, head_count * HD).astype(jnp.bfloat16)
    attended = (
        sum_columns(jnp.dot(context, proj_full, preferred_element_type=jnp.float32)) + proj_bias
    )
    hidden = values + attended
    centered_two, inv_two, normed_two = norm_forward(hidden, gain_two, shift_two)
    mlp_input = spread_features(normed_two)
    pre_act = jnp.dot(mlp_input, up_full, preferred_element_type=jnp.float32) + up_bias
    activated = exact_gelu(pre_act).astype(jnp.bfloat16)
    output = (
        hidden
        + sum_columns(jnp.dot(activated, down_full, preferred_element_type=jnp.float32))
        + down_bias
    )
    kept = (
        centered_one,
        inv_one,
        attn_input,
        query_heads,
        key_heads,
        value_heads,
        context,
        centered_two,
        inv_two,
        mlp_input,
        pre_act,
        activated,
    )
    return (output, kept)


def layer_backward(grad_out, kept, weights, params):
    qkv_full, proj_full, up_full, down_full = weights
    (
        gain_one,
        shift_one,
        query_bias,
        value_bias,
        proj_bias,
        gain_two,
        shift_two,
        up_bias,
        down_bias,
    ) = params
    (
        centered_one,
        inv_one,
        attn_input,
        query_heads,
        key_heads,
        value_heads,
        context,
        centered_two,
        inv_two,
        mlp_input,
        pre_act,
        activated,
    ) = kept
    frame_count = attn_input.shape[0]
    score_scale = 1.0 / math.sqrt(HD)
    grad_down_bias = jnp.sum(grad_out, axis=0)
    down_grad = spread_grads(grad_out.astype(jnp.bfloat16))
    grad_down = jnp.einsum("sf,sd->fd", activated, down_grad, preferred_element_type=jnp.float32)
    grad_act = jnp.einsum("sd,fd->sf", down_grad, down_full, preferred_element_type=jnp.float32)
    unused, gelu_pull = jax.vjp(exact_gelu, pre_act)
    grad_pre = gelu_pull(grad_act)[0]
    grad_up_bias = jnp.sum(grad_pre, axis=0)
    grad_pre_low = grad_pre.astype(jnp.bfloat16)
    grad_up = jnp.einsum("sd,sf->df", mlp_input, grad_pre_low, preferred_element_type=jnp.float32)
    grad_normed_two = sum_grad_columns(
        jnp.einsum("sf,df->sd", grad_pre_low, up_full, preferred_element_type=jnp.float32)
    )
    grad_hidden_norm, grad_gain_two, grad_shift_two = norm_backward(
        grad_normed_two, centered_two, inv_two, gain_two
    )
    grad_hidden = grad_out + grad_hidden_norm
    grad_proj_bias = jnp.sum(grad_hidden, axis=0)
    proj_grad = spread_grads(grad_hidden.astype(jnp.bfloat16))
    grad_proj = jnp.einsum("se,sd->ed", context, proj_grad, preferred_element_type=jnp.float32)
    grad_context = jnp.einsum("sd,ed->se", proj_grad, proj_full, preferred_element_type=jnp.float32)
    grad_context = grad_context.astype(jnp.bfloat16).reshape(query_heads.shape)
    softmax_out = attention_probs(query_heads, key_heads)
    grad_probs = jnp.einsum(
        "qhd,khd->hqk", grad_context, value_heads, preferred_element_type=jnp.float32
    )
    grad_value = jnp.einsum(
        "hqk,qhd->khd",
        softmax_out.astype(jnp.bfloat16),
        grad_context,
        preferred_element_type=jnp.float32,
    )
    grad_scores = softmax_out * (
        grad_probs - jnp.sum(softmax_out * grad_probs, axis=-1, keepdims=True)
    )
    scores_low = grad_scores.astype(jnp.bfloat16)
    grad_query = (
        jnp.einsum("hqk,khd->qhd", scores_low, key_heads, preferred_element_type=jnp.float32)
        * score_scale
    )
    grad_key = (
        jnp.einsum("hqk,qhd->khd", scores_low, query_heads, preferred_element_type=jnp.float32)
        * score_scale
    )
    grad_query = grad_query.reshape(frame_count, -1)
    grad_key = grad_key.reshape(frame_count, -1)
    grad_value = grad_value.reshape(frame_count, -1)
    grad_query_bias = jnp.sum(grad_query, axis=0)
    grad_value_bias = jnp.sum(grad_value, axis=0)
    grad_qkv_low = jnp.stack([grad_query, grad_key, grad_value]).astype(jnp.bfloat16)
    grad_qkv = jnp.einsum(
        "sd,jse->jde", attn_input, grad_qkv_low, preferred_element_type=jnp.float32
    )
    grad_normed_one = sum_grad_columns(
        jnp.einsum("jse,jde->sd", grad_qkv_low, qkv_full, preferred_element_type=jnp.float32)
    )
    grad_in_norm, grad_gain_one, grad_shift_one = norm_backward(
        grad_normed_one, centered_one, inv_one, gain_one
    )
    grad_in = grad_hidden + grad_in_norm
    weight_grads = (grad_qkv, grad_proj, grad_up, grad_down)
    vector_grads = (
        grad_gain_one,
        grad_shift_one,
        grad_query_bias,
        grad_value_bias,
        grad_proj_bias,
        grad_gain_two,
        grad_shift_two,
        grad_up_bias,
        grad_down_bias,
    )
    return (grad_in, weight_grads, vector_grads)


def store_slot(buffer, slot_index, is_valid, value):
    current = lax.dynamic_index_in_dim(buffer, slot_index, 0, keepdims=False)
    return lax.dynamic_update_index_in_dim(
        buffer, jnp.where(is_valid, value, current), slot_index, 0
    )


def reduce_end(weight_acc):
    return (
        lax.psum_scatter(
            weight_acc[0].astype(jnp.bfloat16), "row", scatter_dimension=1, tiled=True
        ).astype(jnp.float32),
        lax.psum_scatter(
            weight_acc[1].astype(jnp.bfloat16), "row", scatter_dimension=1, tiled=True
        ).astype(jnp.float32),
        lax.psum_scatter(
            weight_acc[2].astype(jnp.bfloat16), "row", scatter_dimension=0, tiled=True
        ).astype(jnp.float32),
        lax.psum_scatter(
            weight_acc[3].astype(jnp.bfloat16), "row", scatter_dimension=1, tiled=True
        ).astype(jnp.float32),
    )


def on_device(
    inputs,
    first_gain,
    first_shift,
    qkv_weight,
    query_bias,
    value_bias,
    proj_weight,
    proj_bias,
    second_gain,
    second_shift,
    up_weight,
    up_bias,
    down_weight,
    down_bias,
    cotangent,
    live_clips,
):
    micro_count = inputs.shape[0]
    row_count = inputs.shape[2]
    feature_count = inputs.shape[3]
    section_index = lax.axis_index("pipe")
    weights = (
        lax.all_gather(qkv_weight[0], "row", axis=1, tiled=True),
        lax.all_gather(proj_weight[0], "row", axis=1, tiled=True),
        lax.all_gather(up_weight[0], "row", axis=0, tiled=True),
        lax.all_gather(down_weight[0], "row", axis=1, tiled=True),
    )
    params = (
        first_gain[0],
        first_shift[0],
        query_bias[0],
        value_bias[0],
        proj_bias[0],
        second_gain[0],
        second_shift[0],
        up_bias[0],
        down_bias[0],
    )
    kept_buffers = ()
    zero_rows = jnp.zeros((row_count, feature_count), jnp.bfloat16)
    zero_stack = jnp.zeros((micro_count, row_count, feature_count), jnp.bfloat16)
    own_inputs = inputs[:, 0]

    def forward_tick(state_carry, tick_index):
        received, outputs, layer_inputs, buffers = state_carry
        batch_index = tick_index - section_index
        is_valid = (batch_index >= 0) & (batch_index < micro_count)
        slot_index = jnp.clip(batch_index, 0, micro_count - 1)
        own_input = lax.dynamic_index_in_dim(
            own_inputs, jnp.minimum(tick_index, micro_count - 1), 0, keepdims=False
        )
        layer_input = jnp.where(section_index == 0, own_input, received)
        output, kept = layer_forward(layer_input.astype(jnp.float32), weights, params)
        output_low = output.astype(jnp.bfloat16)
        passed = from_behind(output_low, "pipe", 1)
        outputs = store_slot(outputs, slot_index, is_valid, output_low)
        layer_inputs = store_slot(layer_inputs, slot_index, is_valid, layer_input)
        return ((passed, outputs, layer_inputs, buffers), None)

    tick_range = jnp.arange(micro_count + 1)
    forward_out, unused = lax.scan(
        forward_tick, (zero_rows, zero_stack, zero_stack, kept_buffers), tick_range
    )
    unused_rows, outputs, layer_inputs, kept_buffers = forward_out
    weight_acc = tuple((jnp.zeros(part.shape, jnp.float32) for part in weights))
    vector_acc = tuple((jnp.zeros(part.shape, jnp.float32) for part in params))
    grads_init = jnp.zeros((micro_count, row_count, feature_count), jnp.float32)
    live_rows = live_clips[:, 0]
    cot_rows_all = cotangent[:, 0]

    def backward_tick(state_carry, tick_index):
        received, grads_in, weight_sum, vector_sum = state_carry
        batch_index = micro_count - tick_index - section_index
        is_valid = (batch_index >= 0) & (batch_index < micro_count)
        slot_index = jnp.clip(batch_index, 0, micro_count - 1)
        cot_rows = lax.dynamic_index_in_dim(cot_rows_all, slot_index, 0, keepdims=False).astype(
            jnp.float32
        )
        live_flag = lax.dynamic_index_in_dim(live_rows, slot_index, 0, keepdims=False).astype(
            jnp.float32
        )
        grad_out = jnp.where(
            section_index == 1, cot_rows * live_flag, received.astype(jnp.float32)
        ) * is_valid.astype(jnp.float32)
        stored_input = lax.dynamic_index_in_dim(layer_inputs, slot_index, 0, keepdims=False)
        kept = layer_forward(stored_input.astype(jnp.float32), weights, params)[1]
        grad_in, weight_grads, vector_grads = layer_backward(grad_out, kept, weights, params)
        passed = from_behind(grad_in.astype(jnp.bfloat16), "pipe", -1)
        grads_in = store_slot(grads_in, slot_index, is_valid, grad_in)
        weight_sum = jax.tree.map(jnp.add, weight_sum, weight_grads)
        vector_sum = jax.tree.map(jnp.add, vector_sum, vector_grads)
        return ((passed, grads_in, weight_sum, vector_sum), None)

    backward_out, unused_two = lax.scan(
        backward_tick, (zero_rows, grads_init, weight_acc, vector_acc), tick_range
    )
    unused_grad, grads_in, weight_acc, vector_acc = backward_out
    weight_out = reduce_end(weight_acc)
    split_out = lax.psum((vector_acc[2], vector_acc[3], vector_acc[7]), "row")
    whole_out = lax.psum(
        (vector_acc[0], vector_acc[1], vector_acc[4], vector_acc[5], vector_acc[6], vector_acc[8]),
        ("row", "col"),
    )
    return (
        outputs[None, :, None],
        grads_in[None, :, None],
        whole_out[0][None],
        whole_out[1][None],
        weight_out[0][None],
        split_out[0][None],
        split_out[1][None],
        weight_out[1][None],
        whole_out[2][None],
        whole_out[3][None],
        whole_out[4][None],
        weight_out[2][None],
        split_out[2][None],
        weight_out[3][None],
        whole_out[5][None],
    )


def solution(mesh):
    placed = (
        P(None, "row", "col", None),
        P("pipe", None),
        P("pipe", None),
        P("pipe", None, "row", "col"),
        P("pipe", "col"),
        P("pipe", "col"),
        P("pipe", "col", "row"),
        P("pipe", None),
        P("pipe", None),
        P("pipe", None),
        P("pipe", "row", "col"),
        P("pipe", "col"),
        P("pipe", "col", "row"),
        P("pipe", None),
        P(None, "row", "col", None),
        P(None, "row"),
    )
    return jax.shard_map(
        on_device,
        mesh=mesh,
        in_specs=placed,
        out_specs=(
            P("pipe", None, "row", "col", None),
            P("pipe", None, "row", "col", None),
            P("pipe", None),
            P("pipe", None),
            P("pipe", None, "row", "col"),
            P("pipe", "col"),
            P("pipe", "col"),
            P("pipe", "col", "row"),
            P("pipe", None),
            P("pipe", None),
            P("pipe", None),
            P("pipe", "row", "col"),
            P("pipe", "col"),
            P("pipe", "col", "row"),
            P("pipe", None),
        ),
        check_vma=False,
    )
```

profile of v0, /device:TPU:0, one launch (start us, length us, event | category | flops | bytes accessed | tf_op | source)
XLA Modules:
  0.0 2830.5 jit_solution(8740462381904181484)
XLA Ops:
  61.8 961.5 %while.55 = (s32[]{:T(128)}, bf16[512,512]{1,0:T(8,128)(2,1)S(1)}, bf16[4,512,512]{2,1,0:T(8,128)(2,1)}, bf16[4,512,512]{2,1,0:T(8,128)(2,1)}, pred[]{:T(512)}, ...) while((s32[]{:T(128)}, bf16[512,512]{1,0:T(8,128)(2,1)S(1)}, ...), condition=%wide.region_9.10_spmd, body=%wide.region_0.9_spmd.sunk | while | flops 4413463552 | bytes 122786912 | solution.py:315
  131.7 31.9 %reduce-scatter.18.cloned.1.call-done = f32[512,512]{1,0:T(8,128)} async-done(((f32[1024,512]{1,0:T(8,128)}), f32[512,512]{1,0:T(8,128)}) %reduce-scatter.18.cloned.1.call-update) | async-done | bytes 1048592 | tf_op jit(solution)/shard_map/while/body/eval_jaxpr/reduce_scatter | solution.py:26
  169.0 21.4 all-gather.19.cloned.1.call-done
  205.1 30.9 %reduce-scatter.20.cloned.1.call-done = f32[512,512]{1,0:T(8,128)} async-done(((f32[1024,512]{1,0:T(8,128)}), f32[512,512]{1,0:T(8,128)}) %reduce-scatter.20.cloned.1.call-update) | async-done | bytes 1048592 | tf_op jit(solution)/shard_map/while/body/eval_jaxpr/reduce_scatter | solution.py:26
  324.3 31.9 %reduce-scatter.18.cloned.1.call-done = f32[512,512]{1,0:T(8,128)} async-done(((f32[1024,512]{1,0:T(8,128)}), f32[512,512]{1,0:T(8,128)}) %reduce-scatter.18.cloned.1.call-update) | async-done | bytes 1048592 | tf_op jit(solution)/shard_map/while/body/eval_jaxpr/reduce_scatter | solution.py:26
  397.6 30.9 %reduce-scatter.20.cloned.1.call-done = f32[512,512]{1,0:T(8,128)} async-done(((f32[1024,512]{1,0:T(8,128)}), f32[512,512]{1,0:T(8,128)}) %reduce-scatter.20.cloned.1.call-update) | async-done | bytes 1048592 | tf_op jit(solution)/shard_map/while/body/eval_jaxpr/reduce_scatter | solution.py:26
  516.7 31.9 %reduce-scatter.18.cloned.1.call-done = f32[512,512]{1,0:T(8,128)} async-done(((f32[1024,512]{1,0:T(8,128)}), f32[512,512]{1,0:T(8,128)}) %reduce-scatter.18.cloned.1.call-update) | async-done | bytes 1048592 | tf_op jit(solution)/shard_map/while/body/eval_jaxpr/reduce_scatter | solution.py:26
  590.1 30.9 %reduce-scatter.20.cloned.1.call-done = f32[512,512]{1,0:T(8,128)} async-done(((f32[1024,512]{1,0:T(8,128)}), f32[512,512]{1,0:T(8,128)}) %reduce-scatter.20.cloned.1.call-update) | async-done | bytes 1048592 | tf_op jit(solution)/shard_map/while/body/eval_jaxpr/reduce_scatter | solution.py:26
  709.2 31.9 %reduce-scatter.18.cloned.1.call-done = f32[512,512]{1,0:T(8,128)} async-done(((f32[1024,512]{1,0:T(8,128)}), f32[512,512]{1,0:T(8,128)}) %reduce-scatter.18.cloned.1.call-update) | async-done | bytes 1048592 | tf_op jit(solution)/shard_map/while/body/eval_jaxpr/reduce_scatter | solution.py:26
  746.5 21.4 all-gather.19.cloned.1.call-done
  782.6 30.9 %reduce-scatter.20.cloned.1.call-done = f32[512,512]{1,0:T(8,128)} async-done(((f32[1024,512]{1,0:T(8,128)}), f32[512,512]{1,0:T(8,128)}) %reduce-scatter.20.cloned.1.call-update) | async-done | bytes 1048592 | tf_op jit(solution)/shard_map/while/body/eval_jaxpr/reduce_scatter | solution.py:26
  901.7 31.9 %reduce-scatter.18.cloned.1.call-done = f32[512,512]{1,0:T(8,128)} async-done(((f32[1024,512]{1,0:T(8,128)}), f32[512,512]{1,0:T(8,128)}) %reduce-scatter.18.cloned.1.call-update) | async-done | bytes 1048592 | tf_op jit(solution)/shard_map/while/body/eval_jaxpr/reduce_scatter | solution.py:26
  939.0 21.4 all-gather.19.cloned.1.call-done
  975.1 30.9 %reduce-scatter.20.cloned.1.call-done = f32[512,512]{1,0:T(8,128)} async-done(((f32[1024,512]{1,0:T(8,128)}), f32[512,512]{1,0:T(8,128)}) %reduce-scatter.20.cloned.1.call-update) | async-done | bytes 1048592 | tf_op jit(solution)/shard_map/while/body/eval_jaxpr/reduce_scatter | solution.py:26
  1027.3 1663.7 %while.56 = (s32[]{:T(128)}, bf16[512,512]{1,0:T(8,128)(2,1)}, f32[4,512,512]{2,1,0:T(8,128)}, f32[3,512,256]{1,2,0:T(8,128)}, f32[256,512]{1,0:T(8,128)}, /*ind...) while((s32[]{:T(128)}, bf16[512,512]{1,0:T(8,128)(2,1)}, ...), condition=%wide.region_34.35_spmd.clone, body=%wide.region_10.34_spmd.clone.sunk | while | flops 12016956416 | bytes 501957632 | solution.py:348
  1129.0 31.9 %reduce-scatter.22.cloned.1.call-done = f32[512,512]{1,0:T(8,128)} async-done(((f32[1024,512]{1,0:T(8,128)}), f32[512,512]{1,0:T(8,128)}) %reduce-scatter.22.cloned.1.call-update) | async-done | bytes 1048592 | tf_op jit(solution)/shard_map/while/body/eval_jaxpr/reduce_scatter | solution.py:26
  1218.2 31.9 %reduce-scatter.24.cloned.1.call-done = f32[512,512]{1,0:T(8,128)} async-done(((f32[1024,512]{1,0:T(8,128)}), f32[512,512]{1,0:T(8,128)}) %reduce-scatter.24.cloned.1.call-update) | async-done | bytes 1048592 | tf_op jit(solution)/shard_map/while/body/eval_jaxpr/reduce_scatter | solution.py:34
  1256.2 21.4 all-gather.27.cloned.1.call-done
  1456.8 31.9 %reduce-scatter.22.cloned.1.call-done = f32[512,512]{1,0:T(8,128)} async-done(((f32[1024,512]{1,0:T(8,128)}), f32[512,512]{1,0:T(8,128)}) %reduce-scatter.22.cloned.1.call-update) | async-done | bytes 1048592 | tf_op jit(solution)/shard_map/while/body/eval_jaxpr/reduce_scatter | solution.py:26
  1546.0 31.9 %reduce-scatter.24.cloned.1.call-done = f32[512,512]{1,0:T(8,128)} async-done(((f32[1024,512]{1,0:T(8,128)}), f32[512,512]{1,0:T(8,128)}) %reduce-scatter.24.cloned.1.call-update) | async-done | bytes 1048592 | tf_op jit(solution)/shard_map/while/body/eval_jaxpr/reduce_scatter | solution.py:34
  1584.0 21.4 all-gather.27.cloned.1.call-done
  1784.6 31.9 %reduce-scatter.22.cloned.1.call-done = f32[512,512]{1,0:T(8,128)} async-done(((f32[1024,512]{1,0:T(8,128)}), f32[512,512]{1,0:T(8,128)}) %reduce-scatter.22.cloned.1.call-update) | async-done | bytes 1048592 | tf_op jit(solution)/shard_map/while/body/eval_jaxpr/reduce_scatter | solution.py:26
  1874.0 31.9 %reduce-scatter.24.cloned.1.call-done = f32[512,512]{1,0:T(8,128)} async-done(((f32[1024,512]{1,0:T(8,128)}), f32[512,512]{1,0:T(8,128)}) %reduce-scatter.24.cloned.1.call-update) | async-done | bytes 1048592 | tf_op jit(solution)/shard_map/while/body/eval_jaxpr/reduce_scatter | solution.py:34
  1911.9 21.4 all-gather.27.cloned.1.call-done
  2112.5 31.9 %reduce-scatter.22.cloned.1.call-done = f32[512,512]{1,0:T(8,128)} async-done(((f32[1024,512]{1,0:T(8,128)}), f32[512,512]{1,0:T(8,128)}) %reduce-scatter.22.cloned.1.call-update) | async-done | bytes 1048592 | tf_op jit(solution)/shard_map/while/body/eval_jaxpr/reduce_scatter | solution.py:26
  2201.8 31.9 %reduce-scatter.24.cloned.1.call-done = f32[512,512]{1,0:T(8,128)} async-done(((f32[1024,512]{1,0:T(8,128)}), f32[512,512]{1,0:T(8,128)}) %reduce-scatter.24.cloned.1.call-update) | async-done | bytes 1048592 | tf_op jit(solution)/shard_map/while/body/eval_jaxpr/reduce_scatter | solution.py:34
  2239.7 21.4 all-gather.27.cloned.1.call-done
  2440.3 31.9 %reduce-scatter.22.cloned.1.call-done = f32[512,512]{1,0:T(8,128)} async-done(((f32[1024,512]{1,0:T(8,128)}), f32[512,512]{1,0:T(8,128)}) %reduce-scatter.22.cloned.1.call-update) | async-done | bytes 1048592 | tf_op jit(solution)/shard_map/while/body/eval_jaxpr/reduce_scatter | solution.py:26
  2529.8 31.9 %reduce-scatter.24.cloned.1.call-done = f32[512,512]{1,0:T(8,128)} async-done(((f32[1024,512]{1,0:T(8,128)}), f32[512,512]{1,0:T(8,128)}) %reduce-scatter.24.cloned.1.call-update) | async-done | bytes 1048592 | tf_op jit(solution)/shard_map/while/body/eval_jaxpr/reduce_scatter | solution.py:34
  2567.7 21.4 all-gather.27.cloned.1.call-done
  2716.6 58.3 %all-reduce = (f32[1,512]{1,0:T(1,128)}, f32[1,512]{1,0:T(1,128)}, f32[1,512]{1,0:T(1,128)}, f32[1,512]{1,0:T(1,128)}, f32[1,512]{1,0:T(1,128)}, /*index=5*/f32[1,512]{1,0:T(1,128)}) all-reduce(f32[1,512]{1,0:T(1,128)S(1)} %bitcast.384, f32[1,512]{1,0:T(1,128)S(1)} %bitcast.383, ...), channel_id=1, replica_groups=mesh['pipe'=2,'row'=8,'col'=2] {'row','col'}, use_global_device_ids=true, to_apply=%region_35.36 | all-reduce | flops 3072 | bytes 24576 | tf_op jit(solution)/shard_map/psum | solution.py:354
  2790.4 31.3 %reduce-scatter.16.cloned.1.call-done = bf16[1024,64]{0,1:T(8,128)(2,1)} async-done(((bf16[1024,512]{0,1:T(8,128)(2,1)}), bf16[1024,64]{0,1:T(8,128)(2,1)}) %reduce-scatter.16.cloned.1.call-update) | async-done | bytes 131088 | tf_op jit(solution)/shard_map/reduce_scatter | solution.py:248
  (1395 shorter events, 1879.3 us)
Async XLA Ops:
  68.8 94.9 %reduce-scatter.18.cloned.1.call-start = ((), (), s32[]{:S(2)}) async-start(), calls=%async_computation.16 | async-start | bytes 3145728 | tf_op jit(solution)/shard_map/while/body/eval_jaxpr/reduce_scatter | solution.py:26
  169.0 67.0 %reduce-scatter.20.cloned.1.call-start = ((), (), s32[]{:S(2)}) async-start(), calls=%async_computation.18 | async-start | bytes 3145728 | tf_op jit(solution)/shard_map/while/body/eval_jaxpr/reduce_scatter | solution.py:26
  260.0 96.2 %reduce-scatter.18.cloned.1.call-start = ((), (), s32[]{:S(2)}) async-start(), calls=%async_computation.16 | async-start | bytes 3145728 | tf_op jit(solution)/shard_map/while/body/eval_jaxpr/reduce_scatter | solution.py:26
  361.5 67.0 %reduce-scatter.20.cloned.1.call-start = ((), (), s32[]{:S(2)}) async-start(), calls=%async_computation.18 | async-start | bytes 3145728 | tf_op jit(solution)/shard_map/while/body/eval_jaxpr/reduce_scatter | solution.py:26
  452.5 96.2 %reduce-scatter.18.cloned.1.call-start = ((), (), s32[]{:S(2)}) async-start(), calls=%async_computation.16 | async-start | bytes 3145728 | tf_op jit(solution)/shard_map/while/body/eval_jaxpr/reduce_scatter | solution.py:26
  554.0 67.0 %reduce-scatter.20.cloned.1.call-start = ((), (), s32[]{:S(2)}) async-start(), calls=%async_computation.18 | async-start | bytes 3145728 | tf_op jit(solution)/shard_map/while/body/eval_jaxpr/reduce_scatter | solution.py:26
  645.0 96.2 %reduce-scatter.18.cloned.1.call-start = ((), (), s32[]{:S(2)}) async-start(), calls=%async_computation.16 | async-start | bytes 3145728 | tf_op jit(solution)/shard_map/while/body/eval_jaxpr/reduce_scatter | solution.py:26
  746.5 67.0 %reduce-scatter.20.cloned.1.call-start = ((), (), s32[]{:S(2)}) async-start(), calls=%async_computation.18 | async-start | bytes 3145728 | tf_op jit(solution)/shard_map/while/body/eval_jaxpr/reduce_scatter | solution.py:26
  837.5 96.2 %reduce-scatter.18.cloned.1.call-start = ((), (), s32[]{:S(2)}) async-start(), calls=%async_computation.16 | async-start | bytes 3145728 | tf_op jit(solution)/shard_map/while/body/eval_jaxpr/reduce_scatter | solution.py:26
  939.0 67.0 %reduce-scatter.20.cloned.1.call-start = ((), (), s32[]{:S(2)}) async-start(), calls=%async_computation.18 | async-start | bytes 3145728 | tf_op jit(solution)/shard_map/while/body/eval_jaxpr/reduce_scatter | solution.py:26
  1057.0 103.8 %reduce-scatter.22.cloned.1.call-start = ((), (), s32[]{:S(2)}) async-start(), calls=%async_computation.20 | async-start | bytes 3145728 | tf_op jit(solution)/shard_map/while/body/eval_jaxpr/reduce_scatter | solution.py:26
  1168.0 82.2 %reduce-scatter.24.cloned.1.call-start = ((), (), s32[]{:S(2)}) async-start(), calls=%async_computation.23 | async-start | bytes 3145728 | tf_op jit(solution)/shard_map/while/body/eval_jaxpr/reduce_scatter | solution.py:34
  1218.2 59.4 %all-gather.27.cloned.1.call-start = ((), (), s32[]{:S(2)}) async-start(), calls=%async_computation.24 | async-start | bytes 1572864 | tf_op jit(solution)/shard_map/while/body/eval_jaxpr/all_gather | solution.py:30
  1256.1 102.7 %reduce-scatter.26.cloned.1.call-start = ((), (), s32[]{:S(2)}) async-start(), calls=%async_computation.25 | async-start | bytes 3145728 | tf_op jit(solution)/shard_map/while/body/eval_jaxpr/reduce_scatter | solution.py:34
  1386.7 102.0 %reduce-scatter.22.cloned.1.call-start = ((), (), s32[]{:S(2)}) async-start(), calls=%async_computation.20 | async-start | bytes 3145728 | tf_op jit(solution)/shard_map/while/body/eval_jaxpr/reduce_scatter | solution.py:26
  1495.8 82.2 %reduce-scatter.24.cloned.1.call-start = ((), (), s32[]{:S(2)}) async-start(), calls=%async_computation.23 | async-start | bytes 3145728 | tf_op jit(solution)/shard_map/while/body/eval_jaxpr/reduce_scatter | solution.py:34
  1546.0 59.4 %all-gather.27.cloned.1.call-start = ((), (), s32[]{:S(2)}) async-start(), calls=%async_computation.24 | async-start | bytes 1572864 | tf_op jit(solution)/shard_map/while/body/eval_jaxpr/all_gather | solution.py:30
  1583.9 102.7 %reduce-scatter.26.cloned.1.call-start = ((), (), s32[]{:S(2)}) async-start(), calls=%async_computation.25 | async-start | bytes 3145728 | tf_op jit(solution)/shard_map/while/body/eval_jaxpr/reduce_scatter | solution.py:34
  1714.5 102.0 %reduce-scatter.22.cloned.1.call-start = ((), (), s32[]{:S(2)}) async-start(), calls=%async_computation.20 | async-start | bytes 3145728 | tf_op jit(solution)/shard_map/while/body/eval_jaxpr/reduce_scatter | solution.py:26
  1823.6 82.3 %reduce-scatter.24.cloned.1.call-start = ((), (), s32[]{:S(2)}) async-start(), calls=%async_computation.23 | async-start | bytes 3145728 | tf_op jit(solution)/shard_map/while/body/eval_jaxpr/reduce_scatter | solution.py:34
  1911.9 102.7 %reduce-scatter.26.cloned.1.call-start = ((), (), s32[]{:S(2)}) async-start(), calls=%async_computation.25 | async-start | bytes 3145728 | tf_op jit(solution)/shard_map/while/body/eval_jaxpr/reduce_scatter | solution.py:34
  2042.4 102.0 %reduce-scatter.22.cloned.1.call-start = ((), (), s32[]{:S(2)}) async-start(), calls=%async_computation.20 | async-start | bytes 3145728 | tf_op jit(solution)/shard_map/while/body/eval_jaxpr/reduce_scatter | solution.py:26
  2151.5 82.2 %reduce-scatter.24.cloned.1.call-start = ((), (), s32[]{:S(2)}) async-start(), calls=%async_computation.23 | async-start | bytes 3145728 | tf_op jit(solution)/shard_map/while/body/eval_jaxpr/reduce_scatter | solution.py:34
  2201.7 59.4 %all-gather.27.cloned.1.call-start = ((), (), s32[]{:S(2)}) async-start(), calls=%async_computation.24 | async-start | bytes 1572864 | tf_op jit(solution)/shard_map/while/body/eval_jaxpr/all_gather | solution.py:30
  2239.7 102.7 %reduce-scatter.26.cloned.1.call-start = ((), (), s32[]{:S(2)}) async-start(), calls=%async_computation.25 | async-start | bytes 3145728 | tf_op jit(solution)/shard_map/while/body/eval_jaxpr/reduce_scatter | solution.py:34
  2370.3 102.0 %reduce-scatter.22.cloned.1.call-start = ((), (), s32[]{:S(2)}) async-start(), calls=%async_computation.20 | async-start | bytes 3145728 | tf_op jit(solution)/shard_map/while/body/eval_jaxpr/reduce_scatter | solution.py:26
  2479.3 82.3 %reduce-scatter.24.cloned.1.call-start = ((), (), s32[]{:S(2)}) async-start(), calls=%async_computation.23 | async-start | bytes 3145728 | tf_op jit(solution)/shard_map/while/body/eval_jaxpr/reduce_scatter | solution.py:34
  2567.6 102.7 %reduce-scatter.26.cloned.1.call-start = ((), (), s32[]{:S(2)}) async-start(), calls=%async_computation.25 | async-start | bytes 3145728 | tf_op jit(solution)/shard_map/while/body/eval_jaxpr/reduce_scatter | solution.py:34
  2691.0 83.9 %reduce-scatter.12.cloned.1.call-start = ((), (), s32[]{:S(2)}) async-start(), calls=%async_computation.10 | async-start | bytes 294912 | tf_op jit(solution)/shard_map/reduce_scatter | solution.py:242
  2693.1 83.2 %reduce-scatter.10.cloned.1.call-start = ((), (), s32[]{:S(2)}) async-start(), calls=%async_computation.9 | async-start | bytes 884736 | tf_op jit(solution)/shard_map/reduce_scatter | solution.py:239
  2695.7 93.1 %reduce-scatter.14.cloned.1.call-start = ((), (), s32[]{:S(2)}) async-start(), calls=%async_computation.11 | async-start | bytes 1179648 | tf_op jit(solution)/shard_map/reduce_scatter | solution.py:245
  2698.7 123.0 %reduce-scatter.16.cloned.1.call-start = ((), (), s32[]{:S(2)}) async-start(), calls=%async_computation.12 | async-start | bytes 1179648 | tf_op jit(solution)/shard_map/reduce_scatter | solution.py:248
  (415 other events, 7726.8 us)
Sparse Core Ops, SparseCore 0:
  9.6 26.7 all-gather.14
  131.8 31.8 reduce-scatter.17
  204.1 31.8 reduce-scatter.19
  260.1 22.2 all-gather.16
  324.3 31.8 reduce-scatter.17
  396.6 31.8 reduce-scatter.19
  452.6 22.2 all-gather.16
  516.8 31.8 reduce-scatter.17
  589.1 31.8 reduce-scatter.19
  709.3 31.8 reduce-scatter.17
  781.6 31.8 reduce-scatter.19
  901.8 31.8 reduce-scatter.17
  974.1 31.8 reduce-scatter.19
  1129.0 31.8 reduce-scatter.21
  1218.3 31.8 reduce-scatter.23
  1326.9 31.8 reduce-scatter.25
  1456.8 31.8 reduce-scatter.21
  1546.1 31.8 reduce-scatter.23
  1654.7 31.8 reduce-scatter.25
  1784.6 31.8 reduce-scatter.21
  1874.1 31.8 reduce-scatter.23
  1982.7 31.8 reduce-scatter.25
  2112.6 31.8 reduce-scatter.21
  2201.9 31.8 reduce-scatter.23
  2310.5 31.8 reduce-scatter.25
  2440.4 31.8 reduce-scatter.21
  2529.8 31.8 reduce-scatter.23
  2638.4 31.8 reduce-scatter.25
  2694.3 29.5 reduce-scatter.11
  2726.1 29.6 reduce-scatter.9
  2758.1 30.6 reduce-scatter.13
  2791.1 30.5 reduce-scatter.15
  (29 shorter events, 614.5 us)
where the time goes:
time: 2840 us; the launch traced here: 2830 us
  waiting for transfers between devices  1450 us (51%)
  matrix products  729 us (26%)
  other arithmetic  380 us (13%)
  blocking collectives  109 us (4%)
  local copies, waits for them, and re-layouts  83.2 us (3%)
  loops' own time  42.2 us (1%)
    reduce_scatter x15, waiting for transfers between devices, sum_columns(): lax.psum_scatter(partial_rows, 'col', scatter_dimension=0, tiled=True)  474 us
    all_gather x20, waiting for transfers between devices, spread_features(): return lax.all_gather(normed, 'col', axis=0, tiled=True)  388 us
    reduce_scatter x10, waiting for transfers between devices, sum_grad_columns(): lax.psum_scatter(partial_rows, 'col', scatter_dimension=0, tiled=True)  246 us
    sub x10, other arithmetic, attention_probs(): return jax.nn.softmax(scores, axis=-1)  158 us
    all_gather x10, waiting for transfers between devices, spread_grads(): return lax.all_gather(grad_low, 'col', axis=0, tiled=True)  158 us
    dot_general x10, matrix products, layer_forward(): jnp.einsum('hqk,khd->qhd', softmax_out.astype(jnp.bfloat16), value_heads,...  158 us
    ppermute x10, waiting for transfers between devices, from_behind(): lax.ppermute(value, axis, [(source, source + steps) for source in range(f...  126 us
    dot_general x5, matrix products, layer_backward(): jnp.einsum('qhd,khd->hqk', grad_context, value_heads, preferred_element_t...  82.3 us
  transfers between devices with their start and end apart: 71, of which 68 were waited for; matrix products, arithmetic and copies ran while one was open for 7% of the time, Pallas kernels for 0%

commit v1 on v0

--- a/solution.py
+++ b/solution.py
@@ -8,6 +8,18 @@
 epsilon = 1e-05
 
 
+def collect(x, axis, dim):
+    ways, here = (lax.axis_size(axis), lax.axis_index(axis))
+    grown, reach = (x, 1)
+    while reach < ways:
+        theirs = lax.ppermute(grown, axis, [(d, d ^ reach) for d in range(ways)])
+        mine_first = jnp.concatenate([grown, theirs], axis=dim)
+        theirs_first = jnp.concatenate([theirs, grown], axis=dim)
+        grown = jnp.where(here & reach == 0, mine_first, theirs_first)
+        reach = 2 * reach
+    return grown
+
+
 def from_behind(value, axis, steps):
     count = lax.axis_size(axis)
     first, last = (max(0, -steps), min(count, count - steps))
@@ -19,7 +31,7 @@
 
 
 def spread_features(normed):
-    return lax.all_gather(normed, "col", axis=0, tiled=True)
+    return collect(normed, "col", 0)
 
 
 def sum_columns(partial_rows):

time: 2840 us -> 2620 us (0.923)
  waiting for transfers between devices: 1450 us -> 1200 us
    all_gather x20 -> x0, waiting for transfers between devices: 388 us -> none  [spread_features(): return lax.all_gather(normed, 'col', axis=0, tiled=True)]
    ppermute x0 -> x20, waiting for transfers between devices: none -> 203 us  [collect(): theirs = lax.ppermute(grown, axis, [(d, d ^ reach) for d in range(ways)])]
    all_gather x10, waiting for transfers between devices: 158 us -> 107 us  [spread_grads(): return lax.all_gather(grad_low, 'col', axis=0, tiled=True)]
  transfers between devices with their start and end apart: 71 -> 71, of which waited for: 68 -> 63; matrix products, arithmetic and copies ran while one was open for 7% -> 8% of each run, Pallas kernels for 0% -> 0%
where the time goes in v1:
time: 2620 us
  waiting for transfers between devices  1200 us (46%)
  matrix products  738 us (28%)
  other arithmetic  383 us (15%)
  blocking collectives  109 us (4%)
  local copies, waits for them, and re-layouts  89.5 us (3%)
  loops' own time  41.5 us (2%)
  starting transfers between devices  35.5 us (1%)
    reduce_scatter x15, waiting for transfers between devices, sum_columns(): lax.psum_scatter(partial_rows, 'col', scatter_dimension=0, tiled=True)  475 us
    reduce_scatter x10, waiting for transfers between devices, sum_grad_columns(): lax.psum_scatter(partial_rows, 'col', scatter_dimension=0, tiled=True)  243 us
    ppermute x20, waiting for transfers between devices, collect(): theirs = lax.ppermute(grown, axis, [(d, d ^ reach) for d in range(ways)])  203 us
    sub x10, other arithmetic, attention_probs(): return jax.nn.softmax(scores, axis=-1)  158 us
    dot_general x10, matrix products, layer_forward(): jnp.einsum('hqk,khd->qhd', softmax_out.astype(jnp.bfloat16), value_heads,...  156 us
    ppermute x10, waiting for transfers between devices, from_behind(): lax.ppermute(value, axis, [(source, source + steps) for source in range(f...  124 us
    all_gather x10, waiting for transfers between devices, spread_grads(): return lax.all_gather(grad_low, 'col', axis=0, tiled=True)  107 us
    dot_general x5, matrix products, layer_backward(): jnp.einsum('qhd,khd->hqk', grad_context, value_heads, preferred_element_t...  82.3 us
  transfers between devices with their start and end apart: 71, of which 63 were waited for; matrix products, arithmetic and copies ran while one was open for 8% of the time, Pallas kernels for 0%

profile of v1, /device:TPU:0, one launch (start us, length us, event | category | flops | bytes accessed | tf_op | source)
XLA Modules:
  0.0 2616.2 jit_solution(7384518971983356016)
XLA Ops:
  61.8 875.9 %while.55 = (s32[]{:T(128)}, bf16[512,512]{1,0:T(8,128)(2,1)S(1)}, bf16[4,512,512]{2,1,0:T(8,128)(2,1)}, bf16[4,512,512]{2,1,0:T(8,128)(2,1)}, pred[]{:T(512)}, ...) while((s32[]{:T(128)}, bf16[512,512]{1,0:T(8,128)(2,1)S(1)}, ...), condition=%wide.region_9.10_spmd, body=%wide.region_0.9_spmd.sunk | while | flops 4422900736 | bytes 123835592 | solution.py:327
  124.3 31.6 %reduce-scatter.18.cloned.1.call-done = f32[512,512]{1,0:T(8,128)} async-done(((f32[1024,512]{1,0:T(8,128)}), f32[512,512]{1,0:T(8,128)}) %reduce-scatter.18.cloned.1.call-update) | async-done | bytes 1048592 | tf_op jit(solution)/shard_map/while/body/eval_jaxpr/reduce_scatter | solution.py:38
  189.3 30.9 %reduce-scatter.20.cloned.1.call-done = f32[512,512]{1,0:T(8,128)} async-done(((f32[1024,512]{1,0:T(8,128)}), f32[512,512]{1,0:T(8,128)}) %reduce-scatter.20.cloned.1.call-update) | async-done | bytes 1048592 | tf_op jit(solution)/shard_map/while/body/eval_jaxpr/reduce_scatter | solution.py:38
  298.1 32.9 %reduce-scatter.18.cloned.1.call-done = f32[512,512]{1,0:T(8,128)} async-done(((f32[1024,512]{1,0:T(8,128)}), f32[512,512]{1,0:T(8,128)}) %reduce-scatter.18.cloned.1.call-update) | async-done | bytes 1048592 | tf_op jit(solution)/shard_map/while/body/eval_jaxpr/reduce_scatter | solution.py:38
  364.5 30.9 %reduce-scatter.20.cloned.1.call-done = f32[512,512]{1,0:T(8,128)} async-done(((f32[1024,512]{1,0:T(8,128)}), f32[512,512]{1,0:T(8,128)}) %reduce-scatter.20.cloned.1.call-update) | async-done | bytes 1048592 | tf_op jit(solution)/shard_map/while/body/eval_jaxpr/reduce_scatter | solution.py:38
  473.2 32.9 %reduce-scatter.18.cloned.1.call-done = f32[512,512]{1,0:T(8,128)} async-done(((f32[1024,512]{1,0:T(8,128)}), f32[512,512]{1,0:T(8,128)}) %reduce-scatter.18.cloned.1.call-update) | async-done | bytes 1048592 | tf_op jit(solution)/shard_map/while/body/eval_jaxpr/reduce_scatter | solution.py:38
  539.6 30.9 %reduce-scatter.20.cloned.1.call-done = f32[512,512]{1,0:T(8,128)} async-done(((f32[1024,512]{1,0:T(8,128)}), f32[512,512]{1,0:T(8,128)}) %reduce-scatter.20.cloned.1.call-update) | async-done | bytes 1048592 | tf_op jit(solution)/shard_map/while/body/eval_jaxpr/reduce_scatter | solution.py:38
  648.4 33.0 %reduce-scatter.18.cloned.1.call-done = f32[512,512]{1,0:T(8,128)} async-done(((f32[1024,512]{1,0:T(8,128)}), f32[512,512]{1,0:T(8,128)}) %reduce-scatter.18.cloned.1.call-update) | async-done | bytes 1048592 | tf_op jit(solution)/shard_map/while/body/eval_jaxpr/reduce_scatter | solution.py:38
  714.8 30.9 %reduce-scatter.20.cloned.1.call-done = f32[512,512]{1,0:T(8,128)} async-done(((f32[1024,512]{1,0:T(8,128)}), f32[512,512]{1,0:T(8,128)}) %reduce-scatter.20.cloned.1.call-update) | async-done | bytes 1048592 | tf_op jit(solution)/shard_map/while/body/eval_jaxpr/reduce_scatter | solution.py:38
  823.5 33.0 %reduce-scatter.18.cloned.1.call-done = f32[512,512]{1,0:T(8,128)} async-done(((f32[1024,512]{1,0:T(8,128)}), f32[512,512]{1,0:T(8,128)}) %reduce-scatter.18.cloned.1.call-update) | async-done | bytes 1048592 | tf_op jit(solution)/shard_map/while/body/eval_jaxpr/reduce_scatter | solution.py:38
  889.9 30.9 %reduce-scatter.20.cloned.1.call-done = f32[512,512]{1,0:T(8,128)} async-done(((f32[1024,512]{1,0:T(8,128)}), f32[512,512]{1,0:T(8,128)}) %reduce-scatter.20.cloned.1.call-update) | async-done | bytes 1048592 | tf_op jit(solution)/shard_map/while/body/eval_jaxpr/reduce_scatter | solution.py:38
  940.9 1535.9 %while.56 = (s32[]{:T(128)}, bf16[512,512]{1,0:T(8,128)(2,1)S(1)}, f32[4,512,512]{2,1,0:T(8,128)}, f32[3,512,256]{1,2,0:T(8,128)}, f32[256,512]{1,0:T(8,128)}, /...) while((s32[]{:T(128)}, bf16[512,512]{1,0:T(8,128)(2,1)S(1)}, ...), condition=%wide.region_34.35_spmd.clone, body=%wide.region_10.34_spmd.clone.sunk | while | flops 12035830784 | bytes 494568288 | solution.py:360
  994.2 19.1 fusion.307
  1032.0 32.9 %reduce-scatter.22.cloned.1.call-done = f32[512,512]{1,0:T(8,128)} async-done(((f32[1024,512]{1,0:T(8,128)}), f32[512,512]{1,0:T(8,128)}) %reduce-scatter.22.cloned.1.call-update) | async-done | bytes 1048592 | tf_op jit(solution)/shard_map/while/body/eval_jaxpr/reduce_scatter | solution.py:38
  1106.1 32.0 %reduce-scatter.24.cloned.1.call-done = f32[512,512]{1,0:T(8,128)} async-done(((f32[1024,512]{1,0:T(8,128)}), f32[512,512]{1,0:T(8,128)}) %reduce-scatter.24.cloned.1.call-update) | async-done | bytes 1048592 | tf_op jit(solution)/shard_map/while/body/eval_jaxpr/reduce_scatter | solution.py:46
  1143.9 21.4 all-gather.15.cloned.1.call-done
  1298.4 19.1 fusion.307
  1336.1 31.0 %reduce-scatter.22.cloned.1.call-done = f32[512,512]{1,0:T(8,128)} async-done(((f32[1024,512]{1,0:T(8,128)}), f32[512,512]{1,0:T(8,128)}) %reduce-scatter.22.cloned.1.call-update) | async-done | bytes 1048592 | tf_op jit(solution)/shard_map/while/body/eval_jaxpr/reduce_scatter | solution.py:38
  1408.3 32.0 %reduce-scatter.24.cloned.1.call-done = f32[512,512]{1,0:T(8,128)} async-done(((f32[1024,512]{1,0:T(8,128)}), f32[512,512]{1,0:T(8,128)}) %reduce-scatter.24.cloned.1.call-update) | async-done | bytes 1048592 | tf_op jit(solution)/shard_map/while/body/eval_jaxpr/reduce_scatter | solution.py:46
  1446.1 21.4 all-gather.15.cloned.1.call-done
  1600.6 19.1 fusion.307
  1638.3 31.0 %reduce-scatter.22.cloned.1.call-done = f32[512,512]{1,0:T(8,128)} async-done(((f32[1024,512]{1,0:T(8,128)}), f32[512,512]{1,0:T(8,128)}) %reduce-scatter.22.cloned.1.call-update) | async-done | bytes 1048592 | tf_op jit(solution)/shard_map/while/body/eval_jaxpr/reduce_scatter | solution.py:38
  1710.5 32.0 %reduce-scatter.24.cloned.1.call-done = f32[512,512]{1,0:T(8,128)} async-done(((f32[1024,512]{1,0:T(8,128)}), f32[512,512]{1,0:T(8,128)}) %reduce-scatter.24.cloned.1.call-update) | async-done | bytes 1048592 | tf_op jit(solution)/shard_map/while/body/eval_jaxpr/reduce_scatter | solution.py:46
  1748.3 21.4 all-gather.15.cloned.1.call-done
  1940.5 31.0 %reduce-scatter.22.cloned.1.call-done = f32[512,512]{1,0:T(8,128)} async-done(((f32[1024,512]{1,0:T(8,128)}), f32[512,512]{1,0:T(8,128)}) %reduce-scatter.22.cloned.1.call-update) | async-done | bytes 1048592 | tf_op jit(solution)/shard_map/while/body/eval_jaxpr/reduce_scatter | solution.py:38
  2012.7 32.0 %reduce-scatter.24.cloned.1.call-done = f32[512,512]{1,0:T(8,128)} async-done(((f32[1024,512]{1,0:T(8,128)}), f32[512,512]{1,0:T(8,128)}) %reduce-scatter.24.cloned.1.call-update) | async-done | bytes 1048592 | tf_op jit(solution)/shard_map/while/body/eval_jaxpr/reduce_scatter | solution.py:46
  2050.5 21.4 all-gather.15.cloned.1.call-done
  2242.8 31.0 %reduce-scatter.22.cloned.1.call-done = f32[512,512]{1,0:T(8,128)} async-done(((f32[1024,512]{1,0:T(8,128)}), f32[512,512]{1,0:T(8,128)}) %reduce-scatter.22.cloned.1.call-update) | async-done | bytes 1048592 | tf_op jit(solution)/shard_map/while/body/eval_jaxpr/reduce_scatter | solution.py:38
  2314.9 32.0 %reduce-scatter.24.cloned.1.call-done = f32[512,512]{1,0:T(8,128)} async-done(((f32[1024,512]{1,0:T(8,128)}), f32[512,512]{1,0:T(8,128)}) %reduce-scatter.24.cloned.1.call-update) | async-done | bytes 1048592 | tf_op jit(solution)/shard_map/while/body/eval_jaxpr/reduce_scatter | solution.py:46
  2352.8 21.4 all-gather.15.cloned.1.call-done
  2502.4 58.3 %all-reduce = (f32[1,512]{1,0:T(1,128)}, f32[1,512]{1,0:T(1,128)}, f32[1,512]{1,0:T(1,128)}, f32[1,512]{1,0:T(1,128)}, f32[1,512]{1,0:T(1,128)}, /*index=5*/f32[1,512]{1,0:T(1,128)}) all-reduce(f32[1,512]{1,0:T(1,128)S(1)} %bitcast.353, f32[1,512]{1,0:T(1,128)S(1)} %bitcast.352, ...), channel_id=1, replica_groups=mesh['pipe'=2,'row'=8,'col'=2] {'row','col'}, use_global_device_ids=true, to_apply=%region_35.36 | all-reduce | flops 3072 | bytes 24576 | tf_op jit(solution)/shard_map/psum | solution.py:366
  2576.6 30.7 %reduce-scatter.16.cloned.1.call-done = bf16[1024,64]{0,1:T(8,128)(2,1)} async-done(((bf16[1024,512]{0,1:T(8,128)(2,1)}), bf16[1024,64]{0,1:T(8,128)(2,1)}) %reduce-scatter.16.cloned.1.call-update) | async-done | bytes 131088 | tf_op jit(solution)/shard_map/reduce_scatter | solution.py:260
  (1315 shorter events, 1671.6 us)
Async XLA Ops:
  62.0 93.8 %reduce-scatter.18.cloned.1.call-start = ((), (), s32[]{:S(2)}) async-start(), calls=%async_computation.15 | async-start | bytes 3145728 | tf_op jit(solution)/shard_map/while/body/eval_jaxpr/reduce_scatter | solution.py:38
  124.2 96.0 %reduce-scatter.20.cloned.1.call-start = ((), (), s32[]{:S(2)}) async-start(), calls=%async_computation.16 | async-start | bytes 3145728 | tf_op jit(solution)/shard_map/while/body/eval_jaxpr/reduce_scatter | solution.py:38
  237.1 93.9 %reduce-scatter.18.cloned.1.call-start = ((), (), s32[]{:S(2)}) async-start(), calls=%async_computation.15 | async-start | bytes 3145728 | tf_op jit(solution)/shard_map/while/body/eval_jaxpr/reduce_scatter | solution.py:38
  298.0 97.3 %reduce-scatter.20.cloned.1.call-start = ((), (), s32[]{:S(2)}) async-start(), calls=%async_computation.16 | async-start | bytes 3145728 | tf_op jit(solution)/shard_map/while/body/eval_jaxpr/reduce_scatter | solution.py:38
  412.3 93.9 %reduce-scatter.18.cloned.1.call-start = ((), (), s32[]{:S(2)}) async-start(), calls=%async_computation.15 | async-start | bytes 3145728 | tf_op jit(solution)/shard_map/while/body/eval_jaxpr/reduce_scatter | solution.py:38
  473.2 97.3 %reduce-scatter.20.cloned.1.call-start = ((), (), s32[]{:S(2)}) async-start(), calls=%async_computation.16 | async-start | bytes 3145728 | tf_op jit(solution)/shard_map/while/body/eval_jaxpr/reduce_scatter | solution.py:38
  587.4 93.9 %reduce-scatter.18.cloned.1.call-start = ((), (), s32[]{:S(2)}) async-start(), calls=%async_computation.15 | async-start | bytes 3145728 | tf_op jit(solution)/shard_map/while/body/eval_jaxpr/reduce_scatter | solution.py:38
  648.3 97.4 %reduce-scatter.20.cloned.1.call-start = ((), (), s32[]{:S(2)}) async-start(), calls=%async_computation.16 | async-start | bytes 3145728 | tf_op jit(solution)/shard_map/while/body/eval_jaxpr/reduce_scatter | solution.py:38
  762.6 93.9 %reduce-scatter.18.cloned.1.call-start = ((), (), s32[]{:S(2)}) async-start(), calls=%async_computation.15 | async-start | bytes 3145728 | tf_op jit(solution)/shard_map/while/body/eval_jaxpr/reduce_scatter | solution.py:38
  823.4 97.4 %reduce-scatter.20.cloned.1.call-start = ((), (), s32[]{:S(2)}) async-start(), calls=%async_computation.16 | async-start | bytes 3145728 | tf_op jit(solution)/shard_map/while/body/eval_jaxpr/reduce_scatter | solution.py:38
  963.8 101.2 %reduce-scatter.22.cloned.1.call-start = ((), (), s32[]{:S(2)}) async-start(), calls=%async_computation.17 | async-start | bytes 3145728 | tf_op jit(solution)/shard_map/while/body/eval_jaxpr/reduce_scatter | solution.py:38
  1031.9 63.9 %all-gather.13.cloned.1.call-start = ((), (), s32[]{:S(2)}) async-start(), calls=%async_computation.18 | async-start | bytes 1572864 | tf_op jit(solution)/shard_map/while/body/eval_jaxpr/all_gather | solution.py:42
  1072.1 66.0 %reduce-scatter.24.cloned.1.call-start = ((), (), s32[]{:S(2)}) async-start(), calls=%async_computation.19 | async-start | bytes 3145728 | tf_op jit(solution)/shard_map/while/body/eval_jaxpr/reduce_scatter | solution.py:46
  1143.8 103.6 %reduce-scatter.26.cloned.1.call-start = ((), (), s32[]{:S(2)}) async-start(), calls=%async_computation.21 | async-start | bytes 3145728 | tf_op jit(solution)/shard_map/while/body/eval_jaxpr/reduce_scatter | solution.py:46
  1267.9 99.2 %reduce-scatter.22.cloned.1.call-start = ((), (), s32[]{:S(2)}) async-start(), calls=%async_computation.17 | async-start | bytes 3145728 | tf_op jit(solution)/shard_map/while/body/eval_jaxpr/reduce_scatter | solution.py:38
  1336.1 62.0 %all-gather.13.cloned.1.call-start = ((), (), s32[]{:S(2)}) async-start(), calls=%async_computation.18 | async-start | bytes 1572864 | tf_op jit(solution)/shard_map/while/body/eval_jaxpr/all_gather | solution.py:42
  1374.3 65.9 %reduce-scatter.24.cloned.1.call-start = ((), (), s32[]{:S(2)}) async-start(), calls=%async_computation.19 | async-start | bytes 3145728 | tf_op jit(solution)/shard_map/while/body/eval_jaxpr/reduce_scatter | solution.py:46
  1446.0 103.6 %reduce-scatter.26.cloned.1.call-start = ((), (), s32[]{:S(2)}) async-start(), calls=%async_computation.21 | async-start | bytes 3145728 | tf_op jit(solution)/shard_map/while/body/eval_jaxpr/reduce_scatter | solution.py:46
  1570.1 99.2 %reduce-scatter.22.cloned.1.call-start = ((), (), s32[]{:S(2)}) async-start(), calls=%async_computation.17 | async-start | bytes 3145728 | tf_op jit(solution)/shard_map/while/body/eval_jaxpr/reduce_scatter | solution.py:38
  1676.5 66.0 %reduce-scatter.24.cloned.1.call-start = ((), (), s32[]{:S(2)}) async-start(), calls=%async_computation.19 | async-start | bytes 3145728 | tf_op jit(solution)/shard_map/while/body/eval_jaxpr/reduce_scatter | solution.py:46
  1748.3 103.6 %reduce-scatter.26.cloned.1.call-start = ((), (), s32[]{:S(2)}) async-start(), calls=%async_computation.21 | async-start | bytes 3145728 | tf_op jit(solution)/shard_map/while/body/eval_jaxpr/reduce_scatter | solution.py:46
  1872.3 99.2 %reduce-scatter.22.cloned.1.call-start = ((), (), s32[]{:S(2)}) async-start(), calls=%async_computation.17 | async-start | bytes 3145728 | tf_op jit(solution)/shard_map/while/body/eval_jaxpr/reduce_scatter | solution.py:38
  1940.5 62.0 %all-gather.13.cloned.1.call-start = ((), (), s32[]{:S(2)}) async-start(), calls=%async_computation.18 | async-start | bytes 1572864 | tf_op jit(solution)/shard_map/while/body/eval_jaxpr/all_gather | solution.py:42
  1978.7 66.0 %reduce-scatter.24.cloned.1.call-start = ((), (), s32[]{:S(2)}) async-start(), calls=%async_computation.19 | async-start | bytes 3145728 | tf_op jit(solution)/shard_map/while/body/eval_jaxpr/reduce_scatter | solution.py:46
  2050.5 103.6 %reduce-scatter.26.cloned.1.call-start = ((), (), s32[]{:S(2)}) async-start(), calls=%async_computation.21 | async-start | bytes 3145728 | tf_op jit(solution)/shard_map/while/body/eval_jaxpr/reduce_scatter | solution.py:46
  2174.6 99.2 %reduce-scatter.22.cloned.1.call-start = ((), (), s32[]{:S(2)}) async-start(), calls=%async_computation.17 | async-start | bytes 3145728 | tf_op jit(solution)/shard_map/while/body/eval_jaxpr/reduce_scatter | solution.py:38
  2281.0 66.0 %reduce-scatter.24.cloned.1.call-start = ((), (), s32[]{:S(2)}) async-start(), calls=%async_computation.19 | async-start | bytes 3145728 | tf_op jit(solution)/shard_map/while/body/eval_jaxpr/reduce_scatter | solution.py:46
  2352.7 103.6 %reduce-scatter.26.cloned.1.call-start = ((), (), s32[]{:S(2)}) async-start(), calls=%async_computation.21 | async-start | bytes 3145728 | tf_op jit(solution)/shard_map/while/body/eval_jaxpr/reduce_scatter | solution.py:46
  2476.8 84.0 %reduce-scatter.12.cloned.1.call-start = ((), (), s32[]{:S(2)}) async-start(), calls=%async_computation.10 | async-start | bytes 294912 | tf_op jit(solution)/shard_map/reduce_scatter | solution.py:254
  2478.9 83.2 %reduce-scatter.10.cloned.1.call-start = ((), (), s32[]{:S(2)}) async-start(), calls=%async_computation.9 | async-start | bytes 884736 | tf_op jit(solution)/shard_map/reduce_scatter | solution.py:251
  2481.6 93.4 %reduce-scatter.14.cloned.1.call-start = ((), (), s32[]{:S(2)}) async-start(), calls=%async_computation.11 | async-start | bytes 1179648 | tf_op jit(solution)/shard_map/reduce_scatter | solution.py:257
  2484.5 122.8 %reduce-scatter.16.cloned.1.call-start = ((), (), s32[]{:S(2)}) async-start(), calls=%async_computation.12 | async-start | bytes 1179648 | tf_op jit(solution)/shard_map/reduce_scatter | solution.py:260
  (385 other events, 4986.1 us)
Sparse Core Ops, SparseCore 0:
  9.6 26.7 all-gather.10
  124.4 31.4 reduce-scatter.17
  188.4 31.8 reduce-scatter.19
  298.2 32.8 reduce-scatter.17
  363.5 31.8 reduce-scatter.19
  473.3 32.8 reduce-scatter.17
  538.6 31.8 reduce-scatter.19
  648.4 32.8 reduce-scatter.17
  713.8 31.8 reduce-scatter.19
  823.6 32.8 reduce-scatter.17
  889.0 31.8 reduce-scatter.19
  1032.0 32.8 reduce-scatter.21
  1072.2 22.4 all-gather.12
  1106.1 31.8 reduce-scatter.23
  1215.6 31.8 reduce-scatter.25
  1336.2 30.9 reduce-scatter.21
  1408.4 31.8 reduce-scatter.23
  1517.8 31.8 reduce-scatter.25
  1638.4 30.9 reduce-scatter.21
  1710.6 31.8 reduce-scatter.23
  1820.0 31.8 reduce-scatter.25
  1940.6 30.9 reduce-scatter.21
  1978.9 22.4 all-gather.12
  2012.8 31.8 reduce-scatter.23
  2122.2 31.8 reduce-scatter.25
  2242.8 30.9 reduce-scatter.21
  2315.0 31.8 reduce-scatter.23
  2424.5 31.8 reduce-scatter.25
  2480.4 29.4 reduce-scatter.11
  2512.2 29.7 reduce-scatter.9
  2544.3 30.6 reduce-scatter.13
  2577.2 30.0 reduce-scatter.15
  (9 shorter events, 194.1 us)
